TPU v7x, 256 devices: a whole 4x4x8 slice. The times are simulated.
256 devices in a mesh: dp: 32 (over x_hi, z, core), tensor: 8 (over y, x_lo).
Axes of the slice: x: 4 (x_hi: 2, x_lo: 2; x = x_hi * 2 + x_lo), y: 4, z: 8, core: 2. Of those that a mesh axis runs over, the one named last changes fastest.
Arguments:
- hidden: bfloat16 [65536, 14336], P('dp', 'tensor'), may hold values from -6 to 6
- grad_out: bfloat16 [65536, 4096], P(('dp', 'tensor')), may hold values from -6 to 6
- proj_in: bfloat16 [64, 14336], P(None, 'tensor'), may hold values from -0.046875 to 0.046875
- proj_out: bfloat16 [64, 4096], replicated, may hold values from -0.09375 to 0.09375
- queries: bfloat16 [4096, 4096], P(('dp', 'tensor')), may hold values from -6 to 6
Outputs:
- scores: float32 [4096, 512], P(('dp', 'tensor'))
All inputs are finite; a program needn't handle non-finite values.
Results may differ from a plain program's by a relative error of at most 0.0041.
Values may be sent and summed in bfloat16 or wider, within the bound.
A program may use at most 64 MiB of HBM per device.

v0:
```python
import jax
import jax.numpy as jnp
from jax import lax
from jax.sharding import PartitionSpec as P

SEQ = 128


def body(hidden, grad_out, proj_in, proj_out, queries):
    partial_in = jnp.dot(hidden, proj_in.T, preferred_element_type=jnp.float32)
    local_out = jnp.dot(grad_out, proj_out.T, preferred_element_type=jnp.float32).astype(
        jnp.bfloat16
    )
    gathered = lax.all_gather(local_out, "tensor", axis=0, tiled=True)
    low_rank = partial_in.shape[1]
    sequences = partial_in.shape[0] // SEQ
    outer_sums = jnp.einsum(
        "sti,stj->sij",
        partial_in.reshape(sequences, SEQ, low_rank),
        gathered.astype(jnp.float32).reshape(sequences, SEQ, low_rank),
        precision=lax.Precision.HIGHEST,
    ).reshape(sequences, low_rank * low_rank)
    factor = SEQ ** (-0.5)
    summed = lax.psum(outer_sums, "tensor")
    features = (summed * factor).astype(jnp.bfloat16)
    scores = jnp.dot(
        queries,
        lax.all_gather(features, "dp", axis=0, tiled=True).T,
        preferred_element_type=jnp.float32,
    )
    return scores * (1.0 / low_rank)


def solution(mesh):
    placed = (
        P("dp", "tensor"),
        P(("dp", "tensor"), None),
        P(None, "tensor"),
        P(),
        P(("dp", "tensor"), None),
    )
    return jax.shard_map(
        body, mesh=mesh, in_specs=placed, out_specs=P(("dp", "tensor"), None), check_vma=False
    )
```

profile of v0, /device:TPU:1, one launch (start us, length us, event | category | flops | bytes accessed | tf_op | source)
XLA Modules:
  0.0 228.6 jit_solution(17852875495229143792)
XLA Ops:
  6.5 0.0 copy-start
  6.5 0.0 all-reduce.2.cloned.1.call-start
  6.5 1.6 copy-done
  8.1 1.8 convolution_convert_fusion
  9.9 24.4 %all_gather.6 = bf16[2048,64]{0,1:T(8,128)(2,1)S(1)} all-gather(bf16[256,64]{0,1:T(8,128)(2,1)S(1)} %convolution_convert_fusion), channel_id=1, replica_groups=mesh['dp'=32,'tensor'=8] {'tensor'}, dimensions={0}, use_global_device_ids=true | all-gather | bytes 294912 | tf_op jit(solution)/shard_map/all_gather | solution.py:14
  34.3 0.0 copy-start.1
  34.3 5.4 %convolution_bitcast_fusion = f32[8,16,8,128]{3,2,1,0:T(8,128)S(1)} fusion(bf16[2048,1792]{1,0:T(8,128)(2,1)} %param.5, bf16[64,1792]{1,0:T(8,128)(2,1)} %param.7), kind=kOutput, calls=%fused_computation | convolution fusion | flops 469762048 | bytes 8093696 | tf_op jit(solution)/shard_map/dot_general | solution.py:10
  39.8 0.5 fusion.1
  40.3 0.9 reshape.11
  41.2 0.0 all-reduce.2.cloned.1.call-update
  41.2 0.0 all-gather.2.cloned.1.call-start
  41.3 81.6 %all-reduce.2.cloned.1.call-done = f32[16,4096]{1,0:T(8,128)} async-done(((f32[16,4096]{1,0:T(8,128)}), f32[16,4096]{1,0:T(8,128)}) %all-reduce.2.cloned.1.call-update) | async-done | bytes 262160 | tf_op jit(solution)/shard_map/psum | solution.py:24
  122.8 1.6 multiply_convert_fusion
  124.4 0.0 all-gather.2.cloned.1.call-update
  124.5 93.3 %all-gather.2.cloned.1.call-done = bf16[512,4096]{1,0:T(8,128)(2,1)} async-done(((bf16[16,4096]{1,0:T(8,128)(2,1)}), bf16[512,4096]{1,0:T(8,128)(2,1)}) %all-gather.2.cloned.1.call-update) | async-done | bytes 4194320 | tf_op jit(solution)/shard_map/all_gather | solution.py:28
  217.8 0.0 copy-done.1
  217.8 4.0 %fusion = f32[16,512]{1,0:T(8,128)} fusion(bf16[512,4096]{1,0:T(8,128)(2,1)} %all-gather.2.cloned.1.call-done, bf16[16,4096]{1,0:T(8,128)(2,1)S(1)} %copy-done.1), kind=kOutput, calls=%fused_computation.3 | convolution fusion | flops 67117056 | bytes 4358144 | tf_op jit(solution)/shard_map/dot_general | solution.py:26
Async XLA Ops:
  6.5 1.6 copy-start
  6.5 116.3 %all-reduce.2.cloned.1.call-start = ((), (), s32[]{:S(2)}) async-start(), calls=%async_computation | async-start | bytes 524288 | tf_op jit(solution)/shard_map/psum | solution.py:24
  34.3 183.4 %copy-start.1 = (bf16[16,4096]{1,0:T(8,128)(2,1)S(1)}, bf16[16,4096]{1,0:T(8,128)(2,1)}, u32[]{:S(2)}) copy-start(bf16[16,4096]{1,0:T(8,128)(2,1)} %param.9) | copy-start | bytes 393220
  41.2 176.6 %all-gather.2.cloned.1.call-start = ((), (), s32[]{:S(2)}) async-start(), calls=%async_computation.1 | async-start | bytes 4325376 | tf_op jit(solution)/shard_map/all_gather | solution.py:28
Sparse Core Ops, SparseCore 0:
  41.3 81.4 all-reduce.1
  126.0 91.7 all-gather.1
where the time goes:
time: 229 us
  waiting for transfers between devices  175 us (76%)
  blocking collectives  24.4 us (11%)
  between operations  13.4 us (6%)
  matrix products  11.8 us (5%)
  local copies, waits for them, and re-layouts  2.48 us (1%)
    all_gather x1, waiting for transfers between devices, body(): lax.all_gather(features, 'dp', axis=0, tiled=True)  93.3 us
    psum x1, waiting for transfers between devices, body(): summed = lax.psum(outer_sums, 'tensor')  81.6 us
    all_gather x1, blocking collectives, body(): gathered = lax.all_gather(local_out, 'tensor', axis=0, tiled=True)  24.4 us
    dot_general x1, matrix products, body(): partial_in = jnp.dot(hidden, proj_in.T, preferred_element_type=jnp.float32)  5.43 us
  transfers between devices with their start and end apart: 2, of which 2 were waited for; matrix products, arithmetic and copies ran while one was open for 0% of the time, Pallas kernels for 0%

commit v1 on v0

v1 whole, which is shorter than its diff:
```python
import functools

import jax
import jax.numpy as jnp
from jax import lax
from jax.experimental import pallas as pl
from jax.experimental.pallas import tpu as pltpu
from jax.sharding import PartitionSpec as P

MESH = pl.DeviceIdType.MESH
BF16, F32 = jnp.bfloat16, jnp.float32
SEQ = 128
RANK = 64
LANES = 128
HALF = RANK // 2

ORDER = (5, 4, 3, 7, 2, 6, 1, 0)


def flip(value, mask, bits):
    result = 0
    for bit in range(bits):
        digit = lax.rem(lax.div(value, 1 << bit), 2)
        result = result + (1 << bit) * (1 - digit if (mask >> bit) & 1 else digit)
    return result


def dot_nt(a, b):
    return lax.dot_general(a, b, (((1,), (1,)), ((), ())), preferred_element_type=F32)


def dot_nn(a, b):
    return lax.dot_general(a, b, (((1,), (0,)), ((), ())), preferred_element_type=F32)


def pack_pair(block):
    return jnp.concatenate([block[:SEQ], block[SEQ:]], axis=1)


def kernel(
    hidden, grad_out, proj_in, proj_out, queries, out,
    x_v, g_v, wi_v, wo_v, q_v, rs_send, rs_recv, r_v, f_send, f_recv, feats, s_send, s_recv, perm,
    x_sem, w_sem, rs_ss, rs_rs, q_ss, q_rs, qc_ss, qc_rs, f_ss, f_rs, s_ss, s_rs,
):
    dp, t = lax.axis_index("dp"), lax.axis_index("tensor")
    c, z, xh = lax.rem(dp, 2), lax.rem(lax.div(dp, 2), 8), lax.div(dp, 16)

    def tc_peer(b, k):
        return (dp + 1 - 2 * c if b else dp, flip(t, k, 3))

    def xz_peer(dx, dz):
        x = 1 - xh if dx else xh
        return ((x * 8 + lax.rem(z + dz, 8)) * 2 + c, t)

    tc_all = [(b, k) for b in (0, 1) for k in range(8) if b or k]
    xz_all = [(dx, dz) for dx in (0, 1) for dz in range(8) if dx or dz]

    loads = [pltpu.make_async_copy(proj_in, wi_v, w_sem.at[0])]
    blocks = {}
    for k in ORDER:
        rows = pl.ds(pl.multiple_of(flip(t, k, 3) * 256, 256), 256)
        blocks[k] = pltpu.make_async_copy(hidden.at[rows], x_v.at[k], x_sem.at[k])
    load_wo = pltpu.make_async_copy(proj_out, wo_v, w_sem.at[1])
    load_g = pltpu.make_async_copy(grad_out, g_v, w_sem.at[2])
    load_q = pltpu.make_async_copy(queries, q_v.at[0], w_sem.at[3])
    loads[0].start()
    for k in ORDER:
        blocks[k].start()
    load_wo.start()
    load_g.start()
    load_q.start()

    barrier = pltpu.get_barrier_semaphore()
    for b, k in tc_all:
        pl.semaphore_signal(barrier, inc=1, device_id=tc_peer(b, k), device_id_type=MESH)
    for dx, dz in xz_all:
        pl.semaphore_signal(barrier, inc=1, device_id=xz_peer(dx, dz), device_id_type=MESH)
    pl.semaphore_wait(barrier, len(tc_all) + len(xz_all))

    def remote(src, dst, ss, rs, peer):
        return pltpu.make_async_remote_copy(
            src_ref=src, dst_ref=dst, send_sem=ss, recv_sem=rs, device_id=peer, device_id_type=MESH
        )

    loads[0].wait()
    wi = wi_v[...]
    rs = {}
    own = None
    for k in ORDER:
        blocks[k].wait()
        part = pack_pair(dot_nt(x_v[k], wi))
        if k:
            rs_send[k] = part.astype(BF16)
            rs[k] = remote(rs_send.at[k], rs_recv.at[k], rs_ss.at[k], rs_rs.at[k], tc_peer(0, k))
            rs[k].start()
        else:
            own = part

    load_q.wait()
    qs = {}
    for k in ORDER[:-1]:
        qs[k] = remote(q_v.at[0], q_v.at[k], q_ss.at[k], q_rs.at[k], tc_peer(0, k))
        qs[k].start()
    qc = {0: remote(q_v.at[0], q_v.at[8], qc_ss.at[0], qc_rs.at[0], tc_peer(1, 0))}
    qc[0].start()

    load_wo.wait()
    load_g.wait()
    pout = pack_pair(dot_nt(g_v[...], wo_v[...])).astype(BF16)

    row = lax.broadcasted_iota(jnp.int32, (512, LANES), 0)
    lane = lax.broadcasted_iota(jnp.int32, (512, LANES), 1)
    b_, a_, tl_ = row // 256, (row // 128) % 2, (row // 32) % 4
    dx_, dz_, s_ = (row // 16) % 2, (row // 2) % 8, row % 2
    src_c = (c + b_) % 2
    src_t = (((t // 4) + a_) % 2) * 4 + tl_
    src_xz = ((xh + dx_) % 2) * 8 + (z - dz_ + 8) % 8
    target = src_xz * 32 + src_c * 16 + src_t * 2 + s_
    for block in range(4):
        perm[:, block * LANES : (block + 1) * LANES] = jnp.where(
            target == lane + block * LANES, 1.0, 0.0
        ).astype(BF16)

    total = own
    for k in ORDER[:-1]:
        rs[k].wait_recv()
        total = total + rs_recv[k].astype(F32)
    pin = total.T
    hi = pin.astype(BF16)
    lo = (pin - hi.astype(F32)).astype(BF16)
    r_v[...] = (dot_nn(hi, pout) + dot_nn(lo, pout)) * (SEQ ** -0.5)
    left = lax.broadcasted_iota(jnp.int32, (HALF, LANES), 1) < RANK
    even, odd = r_v[pl.ds(0, HALF, stride=2), :], r_v[pl.ds(1, HALF, stride=2), :]
    f0 = jnp.where(left, even, pltpu.roll(odd, RANK, 1))
    even, odd = r_v[pl.ds(RANK, HALF, stride=2), :], r_v[pl.ds(RANK + 1, HALF, stride=2), :]
    f1 = jnp.where(left, pltpu.roll(even, RANK, 1), odd)
    mine = jnp.concatenate([f0, f1], axis=0).astype(BF16)
    f_send[...] = mine

    fs = {}
    for dx, dz in sorted(xz_all, key=lambda o: -(2 * o[0] + min(o[1], 8 - o[1]))):
        slot = dx * 8 + dz
        fs[slot] = remote(f_send, f_recv.at[slot], f_ss.at[slot], f_rs.at[slot], xz_peer(dx, dz))
        fs[slot].start()

    for k in ORDER[:-1][::-1]:
        qs[k].wait_recv()
        qc[k] = remote(q_v.at[k], q_v.at[8 + k], qc_ss.at[k], qc_rs.at[k], tc_peer(1, 0))
        qc[k].start()

    def spread(slot, block):
        both = block.astype(F32)
        for s in range(2):
            feats[pl.ds(slot * 2 + s, HALF, stride=32), :] = both[s * HALF : (s + 1) * HALF]

    spread(0, mine)
    for slot in list(fs)[::-1]:
        fs[slot].wait_recv()
        spread(slot, f_recv[slot])
    for k in range(8):
        qc[k].wait_recv()

    right = jnp.concatenate(
        [feats[i * 32 : (i + 1) * 32, :].astype(BF16) for i in range(HALF)], axis=1
    )
    scores = dot_nt(q_v[...].reshape(256, 4096), right) * (1.0 / RANK)
    scores = jnp.concatenate([scores, jnp.zeros((256, LANES - 32), F32)], axis=1)
    scores = pltpu.roll(scores, lax.rem(t, 4) * 32, 1)
    s_send[...] = scores.reshape(16, 16, LANES)

    ssd = {}
    for b, k in [(b, k) for k in ORDER for b in (1, 0) if b or k]:
        slot = b * 8 + k
        ssd[slot] = remote(s_send.at[slot], s_recv.at[slot], s_ss.at[slot], s_rs.at[slot], tc_peer(b, k))
        ssd[slot].start()
    for slot in ssd:
        ssd[slot].wait_recv()
    groups = []
    for g in range(4):
        acc = None
        for j in range(4):
            slot = g * 4 + j
            block = s_recv[slot] if slot else s_send[0]
            acc = block if acc is None else acc + block
        groups.append(acc)
    wide = jnp.concatenate(groups, axis=1)
    p1 = wide.astype(BF16)
    rest = wide - p1.astype(F32)
    p2 = rest.astype(BF16)
    p3 = (rest - p2.astype(F32)).astype(BF16)
    placed = dot_nn(jnp.concatenate([p1, p2, p3], axis=0), perm[...])
    out[...] = (placed[:16] + placed[16:32]) + placed[32:]

    for sends in (rs, qs, qc, fs, ssd):
        for copy in sends.values():
            copy.wait_send()


def body(hidden, grad_out, proj_in, proj_out, queries):
    dma = pltpu.SemaphoreType.DMA
    scratch = [
        pltpu.VMEM((8, 256, 1792), BF16),
        pltpu.VMEM((256, 4096), BF16),
        pltpu.VMEM((64, 1792), BF16),
        pltpu.VMEM((64, 4096), BF16),
        pltpu.VMEM((16, 16, 4096), BF16),
        pltpu.VMEM((8, SEQ, LANES), BF16),
        pltpu.VMEM((8, SEQ, LANES), BF16),
        pltpu.VMEM((LANES, LANES), F32),
        pltpu.VMEM((RANK, LANES), BF16),
        pltpu.VMEM((16, RANK, LANES), BF16),
        pltpu.VMEM((HALF * 32, LANES), F32),
        pltpu.VMEM((16, 16, LANES), F32),
        pltpu.VMEM((16, 16, LANES), F32),
        pltpu.VMEM((512, 512), BF16),
        dma((8,)), dma((4,)), dma((8,)), dma((8,)), dma((8,)), dma((8,)),
        dma((8,)), dma((8,)), dma((16,)), dma((16,)), dma((16,)), dma((16,)),
    ]
    return pl.pallas_call(
        kernel,
        out_shape=jax.ShapeDtypeStruct((16, 512), F32),
        in_specs=[pl.BlockSpec(memory_space=pltpu.HBM)] * 5,
        out_specs=pl.BlockSpec(memory_space=pltpu.VMEM),
        scratch_shapes=scratch,
        compiler_params=pltpu.CompilerParams(
            collective_id=0, has_side_effects=True, vmem_limit_bytes=40 << 20
        ),
    )(hidden, grad_out, proj_in, proj_out, queries)


def solution(mesh):
    placed = (
        P("dp", "tensor"),
        P(("dp", "tensor"), None),
        P(None, "tensor"),
        P(),
        P(("dp", "tensor"), None),
    )
    return jax.shard_map(
        body, mesh=mesh, in_specs=placed, out_specs=P(("dp", "tensor"), None), check_vma=False
    )
```

time: 229 us -> 52.8 us (0.23)
  waiting for transfers between devices: 175 us -> 0 us
  Pallas kernels: 0 us -> 44.3 us
  blocking collectives: 24.4 us -> 0 us
  between operations: 13.4 us -> 0.01 us
  matrix products: 11.8 us -> 0 us
  local copies, waits for them, and re-layouts: 2.48 us -> 8.17 us
    all_gather x1 -> x0, waiting for transfers between devices: 93.3 us -> none  [body(): lax.all_gather(features, 'dp', axis=0, tiled=True)]
    psum x1 -> x0, waiting for transfers between devices: 81.6 us -> none  [body(): summed = lax.psum(outer_sums, 'tensor')]
    pallas_call x0 -> x1, Pallas kernels: none -> 44.3 us  [body(): pl.pallas_call(kernel, out_shape=jax.ShapeDtypeStruct((16, 512), F32), in...]
    all_gather x1 -> x0, blocking collectives: 24.4 us -> none  [body(): gathered = lax.all_gather(local_out, 'tensor', axis=0, tiled=True)]
    dot_general x4 -> x0, matrix products: 11.8 us -> none  [the longest x1 5.43 us: body(): partial_in = jnp.dot(hidden, proj_in.T, preferred_element_type=jnp.float32)]
    unnamed x4 -> x11, local copies, waits for them, and re-layouts: 1.59 us -> 8.17 us
  transfers between devices with their start and end apart: 2 -> 0, of which waited for: 2 -> 0; matrix products, arithmetic and copies ran while one was open for 0% -> 0% of each run, Pallas kernels for 0% -> 0%
where the time goes in v1:
time: 52.8 us; the launch traced here: 52.5 us
  Pallas kernels  44.3 us (84%)
  local copies, waits for them, and re-layouts  8.17 us (15%)
    pallas_call x1, Pallas kernels, body(): pl.pallas_call(kernel, out_shape=jax.ShapeDtypeStruct((16, 512), F32), in...  44.3 us
    unnamed x11, local copies, waits for them, and re-layouts  8.17 us

profile of v1, /device:TPU:1, one launch (start us, length us, event | category | flops | bytes accessed | tf_op | source)
XLA Modules:
  0.0 52.5 jit_solution(4075632952261242034)
XLA Ops:
  0.0 0.0 copy-start
  0.0 3.1 %copy-done = bf16[2048,1792]{1,0:T(8,128)(2,1)S(1)} copy-done((bf16[2048,1792]{1,0:T(8,128)(2,1)S(1)}, bf16[2048,1792]{1,0:T(8,128)(2,1)}, u32[]{:S(2)}) %copy-start) | copy-done | bytes 7340056
  3.1 0.0 copy-start.1
  3.1 1.6 %copy-done.1 = bf16[256,4096]{1,0:T(8,128)(2,1)S(1)} copy-done((bf16[256,4096]{1,0:T(8,128)(2,1)S(1)}, bf16[256,4096]{1,0:T(8,128)(2,1)}, u32[]{:S(2)}) %copy-start.1) | copy-done | bytes 2097176
  4.7 0.0 copy-start.2
  4.7 1.0 %copy-done.2 = bf16[64,4096]{1,0:T(8,128)(2,1)S(1)} copy-done((bf16[64,4096]{1,0:T(8,128)(2,1)S(1)}, bf16[64,4096]{1,0:T(8,128)(2,1)}, u32[]{:S(2)}) %copy-start.2) | copy-done | bytes 524312
  5.7 0.0 copy-start.3
  5.7 0.9 %copy-done.3 = bf16[64,1792]{1,0:T(8,128)(2,1)S(1)} copy-done((bf16[64,1792]{1,0:T(8,128)(2,1)S(1)}, bf16[64,1792]{1,0:T(8,128)(2,1)}, u32[]{:S(2)}) %copy-start.3) | copy-done | bytes 229400
  6.7 0.0 copy-start.4
  6.7 0.9 %copy-done.4 = bf16[16,4096]{1,0:T(8,128)(2,1)S(1)} copy-done((bf16[16,4096]{1,0:T(8,128)(2,1)S(1)}, bf16[16,4096]{1,0:T(8,128)(2,1)}, u32[]{:S(2)}) %copy-start.4) | copy-done | bytes 131096
  7.6 44.3 %shard_map.55 = f32[16,512]{1,0:T(8,128)S(1)} custom-call(bf16[2048,1792]{1,0:T(8,128)(2,1)S(1)} %copy-done, bf16[256,4096]{1,0:T(8,128)(2,1)S(1)} %copy-done.1, bf16[64,1792]{1,0:T(8,128)(2,1)S(1)} %copy-done.3, bf16[64,4096]{1,0:T(8,128)(2,1)S(1)} %copy-done.2, bf16[16,4096]{1,0:T(8,128)(2,1)S(1)} %copy-done.4), custom_call_target="tpu_custom_call" | custom-call | tf_op jit(solution)/shard_map/pallas_call | solution.py:219
  51.9 0.6 %copy.7 = f32[16,512]{1,0:T(8,128)} copy(f32[16,512]{1,0:T(8,128)S(1)} %shard_map.55) | data formatting | bytes 65536
Async XLA Ops:
  0.0 3.1 %copy-start = (bf16[2048,1792]{1,0:T(8,128)(2,1)S(1)}, bf16[2048,1792]{1,0:T(8,128)(2,1)}, u32[]{:S(2)}) copy-start(bf16[2048,1792]{1,0:T(8,128)(2,1)} %hidden.1) | copy-start | bytes 22020100
  3.1 1.6 %copy-start.1 = (bf16[256,4096]{1,0:T(8,128)(2,1)S(1)}, bf16[256,4096]{1,0:T(8,128)(2,1)}, u32[]{:S(2)}) copy-start(bf16[256,4096]{1,0:T(8,128)(2,1)} %grad_out.1) | copy-start | bytes 6291460
  4.7 1.0 %copy-start.2 = (bf16[64,4096]{1,0:T(8,128)(2,1)S(1)}, bf16[64,4096]{1,0:T(8,128)(2,1)}, u32[]{:S(2)}) copy-start(bf16[64,4096]{1,0:T(8,128)(2,1)} %proj_out.1) | copy-start | bytes 1572868
  5.7 0.9 %copy-start.3 = (bf16[64,1792]{1,0:T(8,128)(2,1)S(1)}, bf16[64,1792]{1,0:T(8,128)(2,1)}, u32[]{:S(2)}) copy-start(bf16[64,1792]{1,0:T(8,128)(2,1)} %proj_in.1) | copy-start | bytes 688132
  6.7 0.9 %copy-start.4 = (bf16[16,4096]{1,0:T(8,128)(2,1)S(1)}, bf16[16,4096]{1,0:T(8,128)(2,1)}, u32[]{:S(2)}) copy-start(bf16[16,4096]{1,0:T(8,128)(2,1)} %queries.1) | copy-start | bytes 393220

commit v2 on v0

v2 whole, which is shorter than its diff:
```python
import jax
import jax.numpy as jnp
from jax import lax
from jax.experimental import pallas as pl
from jax.experimental.pallas import tpu as pltpu
from jax.sharding import PartitionSpec as P

MESH = pl.DeviceIdType.MESH
BF16, F32 = jnp.bfloat16, jnp.float32
SEQ = 128
RANK = 64
LANES = 128
FF_PART = 1792
D = 4096
HALF_K = RANK * RANK // 2
TILES = HALF_K // LANES
PITCH = 72

ORDER = (5, 4, 3, 7, 2, 6, 1, 0)
EARLY = 4


def flip(value, mask, bits):
    result = 0
    for bit in range(bits):
        digit = lax.rem(lax.div(value, 1 << bit), 2)
        result = result + (1 << bit) * (1 - digit if (mask >> bit) & 1 else digit)
    return result


def dot_nt(a, b):
    return lax.dot_general(a, b, (((1,), (1,)), ((), ())), preferred_element_type=F32)


def dot_nn(a, b):
    return lax.dot_general(a, b, (((1,), (0,)), ((), ())), preferred_element_type=F32)


def kernel(
    hidden, grad_out, proj_in, proj_out, queries, out,
    x_v, g_v, wi_v, wo_v, q_v, rs_send, rs_recv, r_v, f_send, f_recv, feats, s_send, s_recv, perm,
    x_sem, w_sem, rs_ss, rs_rs, q_ss, q_rs, qc_ss, qc_rs, f_ss, f_rs, s_ss, s_rs,
):
    dp, t = lax.axis_index("dp"), lax.axis_index("tensor")
    c, z, xh = lax.rem(dp, 2), lax.rem(lax.div(dp, 2), 8), lax.div(dp, 16)
    y, xl = lax.div(t, 2), lax.rem(t, 2)
    x = xh * 2 + xl

    def tc_peer(b, k):
        return (dp + 1 - 2 * c if b else dp, flip(t, k, 3))

    def at(px, pz):
        return ((lax.div(px, 2) * 8 + pz) * 2 + c, y * 2 + lax.rem(px, 2))

    def ahead(dx, dz):
        return lax.rem(x + dx, 4), lax.rem(z + dz, 8)

    def behind(dx, dz):
        return lax.rem(x + 4 - dx, 4), lax.rem(z + 8 - dz, 8)

    tc_all = [(b, k) for b in (0, 1) for k in range(8) if b or k]
    xz_all = [(dx, dz) for dx in range(4) for dz in range(8) if dx or dz]
    xz_all.sort(key=lambda o: min(o[0], 4 - o[0]) + min(o[1], 8 - o[1]))

    load_wi = pltpu.make_async_copy(proj_in, wi_v.at[0, pl.ds(0, RANK)], w_sem.at[0])
    load_wi2 = pltpu.make_async_copy(proj_in, wi_v.at[1, pl.ds(RANK, RANK)], w_sem.at[4])
    blocks = {}
    for k in ORDER:
        rows = pl.ds(pl.multiple_of(flip(t, k, 3) * 256, 256), 256)
        blocks[k] = pltpu.make_async_copy(hidden.at[rows], x_v.at[k], x_sem.at[k])
    load_wo = pltpu.make_async_copy(proj_out, wo_v, w_sem.at[1])
    load_g = pltpu.make_async_copy(grad_out, g_v, w_sem.at[2])
    mine_k = pl.ds(pl.multiple_of(xl * HALF_K, HALF_K), HALF_K)
    other_k = pl.ds(pl.multiple_of((1 - xl) * HALF_K, HALF_K), HALF_K)
    load_q = pltpu.make_async_copy(queries.at[:, mine_k], q_v.at[0], w_sem.at[3])
    load_wi.start()
    load_wi2.start()
    for k in ORDER[:2]:
        blocks[k].start()

    with jax.named_scope("greet"):
        barrier = pltpu.get_barrier_semaphore()
        greeted = [tc_peer(b, k) for b, k in tc_all]
        greeted += [at(*ahead(dx, dz)) for dx, dz in xz_all if dz or dx == 2]
        greeted.append(at(lax.rem(x + 3 + 2 * xl, 4), z))
        for peer in greeted[::-1]:
            pl.semaphore_signal(barrier, inc=1, device_id=peer, device_id_type=MESH)

    for k in ORDER[2:]:
        blocks[k].start()
    load_wo.start()
    load_g.start()
    load_q.start()

    def remote(src, dst, ss, rs, peer):
        return pltpu.make_async_remote_copy(
            src_ref=src, dst_ref=dst, send_sem=ss, recv_sem=rs, device_id=peer, device_id_type=MESH
        )

    rs = {}

    def project(k):
        blocks[k].wait()
        return dot_nt(x_v[k, :SEQ], wi_v[0]) + dot_nt(x_v[k, SEQ:], wi_v[1])

    def send_part(k):
        rs[k] = remote(rs_send.at[k], rs_recv.at[k], rs_ss.at[k], rs_rs.at[k], tc_peer(0, k))
        rs[k].start()

    with jax.named_scope("hidden_early"):
        wi_v[0, RANK:, :] = jnp.zeros((RANK, FF_PART), BF16)
        wi_v[1, :RANK, :] = jnp.zeros((RANK, FF_PART), BF16)
        load_wi.wait()
        load_wi2.wait()
        for k in ORDER[:EARLY]:
            rs_send[k] = project(k).astype(BF16)
    with jax.named_scope("entry_wait"):
        pl.semaphore_wait(barrier, len(greeted))
    with jax.named_scope("hidden_late"):
        for k in ORDER[:EARLY]:
            send_part(k)
        for k in ORDER[EARLY:-1]:
            rs_send[k] = project(k).astype(BF16)
            send_part(k)
        own = project(0)

    with jax.named_scope("query_send"):
        qs = {}
        for k in ORDER[:-1]:
            part = other_k if k % 2 else mine_k
            qs[k] = remote(queries.at[:, part], q_v.at[k], q_ss.at[k], q_rs.at[k], tc_peer(0, k))
            qs[k].start()
        load_q.wait()
        qc = {0: remote(q_v.at[0], q_v.at[8], qc_ss.at[0], qc_rs.at[0], tc_peer(1, 0))}
        qc[0].start()

    with jax.named_scope("grad_part"):
        load_wo.wait()
        load_g.wait()
        pout = dot_nt(wo_v[...], g_v[...]).astype(BF16)
        pout = jnp.concatenate([pout[:, :SEQ], pout[:, SEQ:]], axis=0)

    with jax.named_scope("places"):
        row = lax.broadcasted_iota(jnp.int32, (512, LANES), 0)
        lane = lax.broadcasted_iota(jnp.int32, (512, LANES), 1)
        b_, k_ = row // 256, (row // 64) % 4
        x_, z_, s_ = (row // 16) % 4, (row // 2) % 8, row % 2
        y_hi, y_lo = ((y // 2) + k_ // 2) % 2, (y + k_) % 2
        src_c = (c + b_) % 2
        src_t = (y_hi * 2 + y_lo) * 2 + x_ % 2
        target = (((x_ // 2) * 8 + z_) * 2 + src_c) * 16 + src_t * 2 + s_
        for block in range(4):
            perm[:, block * LANES : (block + 1) * LANES] = jnp.where(
                target == lane + block * LANES, 1.0, 0.0
            ).astype(BF16)

    with jax.named_scope("part_wait"):
        total = own
        for k in ORDER[:-1]:
            rs[k].wait_recv()
            total = total + rs_recv[k].astype(F32)
    with jax.named_scope("outer"):
        pin = total.T
        hi = pin.astype(BF16)
        lo = (pin - hi.astype(F32)).astype(BF16)
        r_v[...] = (dot_nt(hi, pout) + dot_nt(lo, pout)) * (SEQ ** -0.5)
        left = lax.broadcasted_iota(jnp.int32, (RANK // 2, LANES), 1) < RANK
        even, odd = r_v[pl.ds(0, 32, stride=2), :], r_v[pl.ds(1, 32, stride=2), :]
        f0 = jnp.where(left, even, pltpu.roll(odd, RANK, 1)).astype(BF16)
        even, odd = r_v[pl.ds(RANK, 32, stride=2), :], r_v[pl.ds(RANK + 1, 32, stride=2), :]
        f1 = jnp.where(left, pltpu.roll(even, RANK, 1), odd).astype(BF16)
        for half in range(2):
            cut = slice(half * TILES, (half + 1) * TILES)
            f_send[half, :TILES] = f0[cut]
            f_send[half, TILES:] = f1[cut]

    with jax.named_scope("feature_send"):
        fs = {}
        for n, (dx, dz) in reversed(list(enumerate(xz_all))):
            px, pz = ahead(dx, dz)
            src = f_send.at[lax.rem(xl + dx, 2)]
            fs[n] = remote(src, f_recv.at[n], f_ss.at[n], f_rs.at[n], at(px, pz))
            fs[n].start()

    with jax.named_scope("query_core"):
        for k in ORDER[:-1][::-1]:
            qs[k].wait_recv()
            qc[k] = remote(q_v.at[k], q_v.at[8 + k], qc_ss.at[k], qc_rs.at[k], tc_peer(1, 0))
            qc[k].start()

    def spread(px, pz, block):
        both = block.astype(F32)
        for s in range(2):
            first = (px * 8 + pz) * 2 + s
            feats[pl.ds(first, TILES, stride=PITCH), :] = both[s * TILES : (s + 1) * TILES]

    with jax.named_scope("feature_wait"):
        spread(x, z, f_send[xl])
        for n, (dx, dz) in enumerate(xz_all):
            fs[n].wait_recv()
            spread(*behind(dx, dz), f_recv[n])
    with jax.named_scope("query_wait"):
        for k in range(8):
            qc[k].wait_recv()

    with jax.named_scope("score_dot"):
        right = jnp.concatenate(
            [feats[i * PITCH : i * PITCH + 64, :].astype(BF16) for i in range(TILES)], axis=1
        )
        scores = dot_nt(q_v[...].reshape(256, HALF_K), right) * (1.0 / RANK)
        scores = scores.reshape(16, 2, 8, 64)
        s_send[...] = jnp.concatenate([scores[:, 0], scores[:, 1]], axis=2)

    with jax.named_scope("score_send"):
        ssd = {}
        for b, k in [(b, k) for k in ORDER for b in (1, 0) if b or k]:
            slot = b * 8 + k
            ssd[slot] = remote(
                s_send.at[slot], s_recv.at[slot], s_ss.at[slot], s_rs.at[slot], tc_peer(b, k)
            )
            ssd[slot].start()
    with jax.named_scope("score_wait"):
        for slot in ssd:
            ssd[slot].wait_recv()
    with jax.named_scope("place"):
        left = lax.broadcasted_iota(jnp.int32, (8, LANES), 1) < 64
        upper, lower = [], []
        for g in range(4):
            pair = []
            for j in range(2):
                slot = g * 4 + j * 2
                first = s_recv[slot] if slot else s_send[0]
                pair.append(first + s_recv[slot + 1])
            upper.append(jnp.where(left, pair[0], pltpu.roll(pair[1], 64, 1)))
            lower.append(jnp.where(left, pltpu.roll(pair[0], 64, 1), pair[1]))
        wide = jnp.concatenate(
            [jnp.concatenate(upper, axis=1), jnp.concatenate(lower, axis=1)], axis=0
        )
        p1 = wide.astype(BF16)
        rest = wide - p1.astype(F32)
        p2 = rest.astype(BF16)
        p3 = (rest - p2.astype(F32)).astype(BF16)
        placed = dot_nn(jnp.concatenate([p1, p2, p3], axis=0), perm[...])
        out[...] = (placed[:16] + placed[16:32]) + placed[32:]

    with jax.named_scope("send_wait"):
        for sends in (rs, qs, qc, fs, ssd):
            for copy in sends.values():
                copy.wait_send()


def body(hidden, grad_out, proj_in, proj_out, queries):
    dma = pltpu.SemaphoreType.DMA
    scratch = [
        pltpu.VMEM((8, 256, FF_PART), BF16),
        pltpu.VMEM((256, D), BF16),
        pltpu.VMEM((2, LANES, FF_PART), BF16),
        pltpu.VMEM((RANK, D), BF16),
        pltpu.VMEM((16, 16, HALF_K), BF16),
        pltpu.VMEM((8, SEQ, LANES), BF16),
        pltpu.VMEM((8, SEQ, LANES), BF16),
        pltpu.VMEM((LANES, LANES), F32),
        pltpu.VMEM((2, 2 * TILES, LANES), BF16),
        pltpu.VMEM((31, 2 * TILES, LANES), BF16),
        pltpu.VMEM((TILES * PITCH, LANES), F32),
        pltpu.VMEM((16, 8, LANES), F32),
        pltpu.VMEM((16, 8, LANES), F32),
        pltpu.VMEM((512, 512), BF16),
        dma((8,)), dma((5,)), dma((8,)), dma((8,)), dma((8,)), dma((8,)),
        dma((8,)), dma((8,)), dma((31,)), dma((31,)), dma((16,)), dma((16,)),
    ]
    return pl.pallas_call(
        kernel,
        out_shape=jax.ShapeDtypeStruct((16, 512), F32),
        in_specs=[pl.BlockSpec(memory_space=pltpu.HBM)] * 5,
        out_specs=pl.BlockSpec(memory_space=pltpu.VMEM),
        scratch_shapes=scratch,
        compiler_params=pltpu.CompilerParams(
            collective_id=0, has_side_effects=True, vmem_limit_bytes=56418304
        ),
    )(hidden, grad_out, proj_in, proj_out, queries)


def solution(mesh):
    placed = (
        P("dp", "tensor"),
        P(("dp", "tensor"), None),
        P(None, "tensor"),
        P(),
        P(("dp", "tensor"), None),
    )
    return jax.shard_map(
        body, mesh=mesh, in_specs=placed, out_specs=P(("dp", "tensor"), None), check_vma=False
    )
```

time: 229 us -> 33.1 us (0.14)
  waiting for transfers between devices: 175 us -> 0 us
  Pallas kernels: 0 us -> 32.4 us
  blocking collectives: 24.4 us -> 0 us
  between operations: 13.4 us -> 0.01 us
  matrix products: 11.8 us -> 0 us
    all_gather x1 -> x0, waiting for transfers between devices: 93.3 us -> none  [body(): lax.all_gather(features, 'dp', axis=0, tiled=True)]
    psum x1 -> x0, waiting for transfers between devices: 81.6 us -> none  [body(): summed = lax.psum(outer_sums, 'tensor')]
    pallas_call x0 -> x1, Pallas kernels: none -> 32.4 us  [body(): pl.pallas_call(kernel, out_shape=jax.ShapeDtypeStruct((16, 512), F32), in...]
    all_gather x1 -> x0, blocking collectives: 24.4 us -> none  [body(): gathered = lax.all_gather(local_out, 'tensor', axis=0, tiled=True)]
    dot_general x4 -> x0, matrix products: 11.8 us -> none  [the longest x1 5.43 us: body(): partial_in = jnp.dot(hidden, proj_in.T, preferred_element_type=jnp.float32)]
  transfers between devices with their start and end apart: 2 -> 0, of which waited for: 2 -> 0; matrix products, arithmetic and copies ran while one was open for 0% -> 0% of each run, Pallas kernels for 0% -> 0%
where the time goes in v2:
time: 33.1 us; the launch traced here: 33 us
  Pallas kernels  32.4 us (98%)
  local copies, waits for them, and re-layouts  0.62 us (2%)
    pallas_call x1, Pallas kernels, body(): pl.pallas_call(kernel, out_shape=jax.ShapeDtypeStruct((16, 512), F32), in...  32.4 us

profile of v2, /device:TPU:1, one launch (start us, length us, event | category | flops | bytes accessed | tf_op | source)
XLA Modules:
  0.0 33.0 jit_solution(7494341503884810154)
XLA Ops:
  0.0 32.4 %shard_map.55 = f32[16,512]{1,0:T(8,128)S(1)} custom-call(bf16[2048,1792]{1,0:T(8,128)(2,1)} %hidden.1, bf16[256,4096]{1,0:T(8,128)(2,1)} %grad_out.1, bf16[64,1792]{1,0:T(8,128)(2,1)} %proj_in.1, bf16[64,4096]{1,0:T(8,128)(2,1)} %proj_out.1, bf16[16,4096]{1,0:T(8,128)(2,1)} %queries.1), custom_call_target="tpu_custom_call" | custom-call | tf_op jit(solution)/shard_map/pallas_call | solution.py:272
  32.4 0.6 %copy.7 = f32[16,512]{1,0:T(8,128)} copy(f32[16,512]{1,0:T(8,128)S(1)} %shard_map.55) | data formatting | bytes 65536

commit v3 on v0

v3 whole, which is shorter than its diff:
```python
import jax
import jax.numpy as jnp
from jax import lax
from jax.experimental import pallas as pl
from jax.experimental.pallas import tpu as pltpu
from jax.sharding import PartitionSpec as P

MESH = pl.DeviceIdType.MESH
BF16, F32 = jnp.bfloat16, jnp.float32
SEQ = 128
RANK = 64
LANES = 128
FF_PART = 1792
D = 4096
HALF_K = RANK * RANK // 2
TILES = HALF_K // LANES
PITCH = 72

ORDER = (5, 4, 3, 7, 2, 6, 1, 0)
STEPS = ((0, ORDER[:4]), (0, ORDER[4:]), (1, ORDER[:4]), (1, ORDER[4:]))
SLOTS = ((0, 0), (0, 1), (1, 0), (3, 0), (1, 1), (3, 1), (2, 0), (2, 1))


def flip(value, mask, bits):
    result = 0
    for bit in range(bits):
        digit = lax.rem(lax.div(value, 1 << bit), 2)
        result = result + (1 << bit) * (1 - digit if (mask >> bit) & 1 else digit)
    return result


def dot_nt(a, b):
    return lax.dot_general(a, b, (((1,), (1,)), ((), ())), preferred_element_type=F32)


def dot_nn(a, b):
    return lax.dot_general(a, b, (((1,), (0,)), ((), ())), preferred_element_type=F32)


def kernel(
    hidden, grad_out, proj_in, proj_out, queries, out,
    x_v, g_v, wi_v, wo_v, q_v, q_o, rs_send, rs_recv, r_v, f_send, f_recv, feats, s_send, s_recv, perm,
    x_sem, w_sem, rs_ss, rs_rs, q_ss, q_rs, qc_ss, qc_rs, f_ss, f_rs, s_ss, s_rs, wave,
):
    dp, t = lax.axis_index("dp"), lax.axis_index("tensor")
    c, z, xh = lax.rem(dp, 2), lax.rem(lax.div(dp, 2), 8), lax.div(dp, 16)
    y, xl = lax.div(t, 2), lax.rem(t, 2)
    x = xh * 2 + xl

    def t_peer(k):
        return (dp, flip(t, k, 3))

    def tc_peer(b, dy, kx):
        return (dp + 1 - 2 * c if b else dp, lax.rem(y + dy, 4) * 2 + (1 - xl if kx else xl))

    def at(px, pz):
        return ((lax.div(px, 2) * 8 + pz) * 2 + c, y * 2 + lax.rem(px, 2))

    def ahead(dx, dz):
        return lax.rem(x + dx, 4), lax.rem(z + dz, 8)

    def behind(dx, dz):
        return lax.rem(x + 4 - dx, 4), lax.rem(z + 8 - dz, 8)

    tc_all = [(b, *o) for b in (0, 1) for o in SLOTS if b or o != (0, 0)]
    tc_all.sort(key=lambda o: -2 * (min(o[1], 4 - o[1]) + o[2]) - o[0])
    xz_all = [(dx, dz) for dx in range(4) for dz in range(8) if dx or dz]
    xz_all.sort(key=lambda o: -min(o[0], 4 - o[0]) - min(o[1], 8 - o[1]))

    def remote(src, dst, ss, rs, peer):
        return pltpu.make_async_remote_copy(
            src_ref=src, dst_ref=dst, send_sem=ss, recv_sem=rs, device_id=peer, device_id_type=MESH
        )

    def settle(ref, sem):
        pltpu.make_async_copy(ref, ref, sem).wait()

    def tell(sem, peer):
        pl.semaphore_signal(sem, inc=1, device_id=peer, device_id_type=MESH)

    mine_k = pl.ds(pl.multiple_of(xl * HALF_K, HALF_K), HALF_K)
    other_k = pl.ds(pl.multiple_of((1 - xl) * HALF_K, HALF_K), HALF_K)
    load_wi = pltpu.make_async_copy(proj_in, wi_v, w_sem.at[0])
    load_wo = pltpu.make_async_copy(proj_out, wo_v, w_sem.at[1])
    load_g = pltpu.make_async_copy(grad_out, g_v, w_sem.at[2])
    load_q = pltpu.make_async_copy(queries.at[:, mine_k], q_v.at[0], w_sem.at[3])
    load_o = pltpu.make_async_copy(queries.at[:, other_k], q_o, w_sem.at[4])

    def load_step(step):
        s, ks = STEPS[step]
        for n, k in enumerate(ks):
            rows = pl.ds(pl.multiple_of(flip(t, k, 3) * 256 + s * SEQ, SEQ), SEQ)
            pltpu.make_async_copy(hidden.at[rows], x_v.at[step, n], x_sem.at[step]).start()

    load_q.start()
    load_o.start()
    load_wi.start()
    load_step(0)

    with jax.named_scope("greet"):
        barrier = pltpu.get_barrier_semaphore()
        greeted = [tc_peer(0, *o) for o in SLOTS[:0:-1]]
        greeted += [at(*ahead(0, dz)) for dz in (2, 6, 1, 7)] + [at(*ahead(2, 0))]
        greeted += [at(lax.rem(x + 3 + 2 * xl, 4), z), tc_peer(1, 0, 0)]
        for peer in greeted:
            tell(barrier, peer)

    for step in range(1, 4):
        load_step(step)
    load_wo.start()
    load_g.start()

    with jax.named_scope("entry_wait"):
        pl.semaphore_wait(barrier, len(greeted))

    with jax.named_scope("heard_0"):
        for dz in (2, 6, 1, 7):
            tell(wave.at[1], at(*ahead(0, dz)))
        tell(wave.at[0], tc_peer(1, 0, 0))

    with jax.named_scope("query_send"):
        load_q.wait()
        load_o.wait()
        remote(q_v.at[0], q_v.at[8], qc_ss, qc_rs, tc_peer(1, 0, 0)).start()
        remote(q_o, q_v.at[1], q_ss, q_rs.at[0], tc_peer(0, 0, 1)).start()
        remote(q_v.at[0], q_v.at[3], q_ss, q_rs.at[1], tc_peer(0, 1, 0)).start()
        remote(q_v.at[0], q_v.at[2], q_ss, q_rs.at[1], tc_peer(0, 3, 0)).start()

    own = {}

    def project(step):
        s, ks = STEPS[step]
        settle(x_v.at[step], x_sem.at[step])
        parts = dot_nt(wi_v[...], x_v[step].reshape(4 * SEQ, FF_PART))
        for n, k in enumerate(ks):
            part = parts[:, n * SEQ : (n + 1) * SEQ]
            if k:
                rs_send[s, k] = part.astype(BF16)
            else:
                own[s] = part

    def send_parts(step):
        s, ks = STEPS[step]
        for k in ks:
            if k:
                remote(rs_send.at[s, k], rs_recv.at[s, k], rs_ss, rs_rs.at[s], t_peer(k)).start()

    load_wi.wait()
    with jax.named_scope("hidden_0"):
        project(0)
        send_parts(0)
    with jax.named_scope("hidden_1"):
        project(1)
        send_parts(1)
    with jax.named_scope("hidden_2"):
        project(2)
        send_parts(2)
    with jax.named_scope("hidden_3"):
        project(3)
        send_parts(3)

    with jax.named_scope("heard_1"):
        pl.semaphore_wait(wave.at[1], 4)
        for dz in (4, 3, 5):
            tell(wave.at[2], at(*ahead(0, dz)))
    with jax.named_scope("query_2"):
        settle(q_v.at[1], q_rs.at[0])
        remote(q_v.at[1], q_v.at[5], q_ss, q_rs.at[2], tc_peer(0, 1, 0)).start()
        remote(q_v.at[1], q_v.at[4], q_ss, q_rs.at[2], tc_peer(0, 3, 0)).start()
    with jax.named_scope("grad_part"):
        load_wo.wait()
        load_g.wait()
        pout = dot_nt(wo_v[...], g_v[...]).astype(BF16)

    with jax.named_scope("heard_2"):
        pl.semaphore_wait(wave.at[0], 1)
        pl.semaphore_wait(wave.at[2], 3)

    def features(s):
        with jax.named_scope("part_wait_%d" % s):
            settle(rs_recv.at[s, pl.ds(1, 7)], rs_rs.at[s])
        with jax.named_scope("outer"):
            pin = own[s]
            for k in range(1, 8):
                pin = pin + rs_recv[s, k].astype(F32)
            hi = pin.astype(BF16)
            lo = (pin - hi.astype(F32)).astype(BF16)
            right = pout[:, s * SEQ : (s + 1) * SEQ]
            twice = jnp.concatenate([right, right], axis=0)
            r_v[...] = (dot_nt(hi, twice) + dot_nt(lo, twice)) * (SEQ ** -0.5)
            left = lax.broadcasted_iota(jnp.int32, (RANK // 2, LANES), 1) < RANK
            even, odd = r_v[pl.ds(0, 32, stride=2), :], r_v[pl.ds(1, 32, stride=2), :]
            f = jnp.where(left, even, odd).astype(BF16)
            f_send[s, 0] = f[:TILES]
            f_send[s, 1] = f[TILES:]
        with jax.named_scope("feature_send_%d" % s):
            for n, (dx, dz) in enumerate(xz_all):
                src = f_send.at[s, lax.rem(xl + dx, 2)]
                remote(src, f_recv.at[s, n], f_ss, f_rs, at(*ahead(dx, dz))).start()

    features(0)
    features(1)
    with jax.named_scope("query_3"):
        first, last = pl.ds(0, HALF_K // 2), pl.ds(HALF_K // 2, HALF_K // 2)
        for kx in range(2):
            settle(q_v.at[pl.ds(2 + 2 * kx, 2)], q_rs.at[1 + kx])
            for slot, part, dy in ((3, first, 1), (2, last, 3)):
                remote(
                    q_v.at[slot + 2 * kx, :, part], q_v.at[6 + kx, :, part], q_ss, q_rs.at[3],
                    tc_peer(0, dy, 0),
                ).start()
        remote(q_v.at[pl.ds(1, 5)], q_v.at[pl.ds(9, 5)], qc_ss, qc_rs, tc_peer(1, 0, 0)).start()

    with jax.named_scope("places"):
        row = lax.broadcasted_iota(jnp.int32, (512, LANES), 0)
        lane = lax.broadcasted_iota(jnp.int32, (512, LANES), 1)
        b_, dy_ = row // 256, (row // 64) % 4
        x_, z_, s_ = (row // 16) % 4, (row // 2) % 8, row % 2
        src_c = (c + b_) % 2
        src_t = ((y + dy_) % 4) * 2 + x_ % 2
        target = (((x_ // 2) * 8 + z_) * 2 + src_c) * 16 + src_t * 2 + s_
        for block in range(4):
            perm[:, block * LANES : (block + 1) * LANES] = jnp.where(
                target == lane + block * LANES, 1.0, 0.0
            ).astype(BF16)

    with jax.named_scope("query_core"):
        settle(q_v.at[pl.ds(6, 2)], q_rs.at[3])
        remote(q_v.at[pl.ds(6, 2)], q_v.at[pl.ds(14, 2)], qc_ss, qc_rs, tc_peer(1, 0, 0)).start()

    def spread(px, pz, s, block):
        feats[pl.ds((px * 8 + pz) * 2 + s, TILES, stride=PITCH), :] = block.astype(F32)

    with jax.named_scope("feature_wait"):
        settle(f_recv, f_rs)
    with jax.named_scope("spread"):
        for s in range(2):
            spread(x, z, s, f_send[s, xl])
            for n, (dx, dz) in enumerate(xz_all):
                spread(*behind(dx, dz), s, f_recv[s, n])
    with jax.named_scope("query_wait"):
        settle(q_v.at[pl.ds(8, 8)], qc_rs)

    with jax.named_scope("score_dot"):
        right = jnp.concatenate(
            [feats[i * PITCH : i * PITCH + 64, :].astype(BF16) for i in range(TILES)], axis=1
        )
        scores = dot_nt(q_v[...].reshape(256, HALF_K), right) * (1.0 / RANK)
        scores = scores.reshape(16, 2, 8, 64)
        s_send[...] = jnp.concatenate([scores[:, 0], scores[:, 1]], axis=2)

    with jax.named_scope("score_send"):
        for b, dy, kx in tc_all:
            slot = b * 8 + SLOTS.index((dy, kx))
            there = b * 8 + SLOTS.index(((4 - dy) % 4, kx))
            remote(s_send.at[slot], s_recv.at[there], s_ss, s_rs, tc_peer(b, dy, kx)).start()
    with jax.named_scope("score_wait"):
        settle(s_recv.at[pl.ds(1, 15)], s_rs)
    with jax.named_scope("place"):
        left = lax.broadcasted_iota(jnp.int32, (8, LANES), 1) < 64
        upper, lower = [], []
        for g in range(4):
            pair = []
            for dy in range(2 * (g % 2), 2 * (g % 2) + 2):
                one, two = [(g // 2) * 8 + SLOTS.index((dy, kx)) for kx in range(2)]
                pair.append((s_recv[one] if one else s_send[0]) + s_recv[two])
            upper.append(jnp.where(left, pair[0], pltpu.roll(pair[1], 64, 1)))
            lower.append(jnp.where(left, pltpu.roll(pair[0], 64, 1), pair[1]))
        wide = jnp.concatenate(
            [jnp.concatenate(upper, axis=1), jnp.concatenate(lower, axis=1)], axis=0
        )
        p1 = wide.astype(BF16)
        rest = wide - p1.astype(F32)
        p2 = rest.astype(BF16)
        p3 = (rest - p2.astype(F32)).astype(BF16)
        placed = dot_nn(jnp.concatenate([p1, p2, p3], axis=0), perm[...])
        out[...] = (placed[:16] + placed[16:32]) + placed[32:]

    with jax.named_scope("send_wait"):
        settle(rs_send.at[:, pl.ds(1, 7)], rs_ss)
        settle(q_v.at[pl.ds(0, 7)], q_ss)
        settle(q_v.at[pl.ds(0, 8)], qc_ss)
        settle(f_recv, f_ss)
        settle(s_send.at[pl.ds(1, 15)], s_ss)


def body(hidden, grad_out, proj_in, proj_out, queries):
    dma = pltpu.SemaphoreType.DMA
    scratch = [
        pltpu.VMEM((4, 4, SEQ, FF_PART), BF16),
        pltpu.VMEM((256, D), BF16),
        pltpu.VMEM((RANK, FF_PART), BF16),
        pltpu.VMEM((RANK, D), BF16),
        pltpu.VMEM((16, 16, HALF_K), BF16),
        pltpu.VMEM((16, HALF_K), BF16),
        pltpu.VMEM((2, 8, RANK, SEQ), BF16),
        pltpu.VMEM((2, 8, RANK, SEQ), BF16),
        pltpu.VMEM((RANK, LANES), F32),
        pltpu.VMEM((2, 2, TILES, LANES), BF16),
        pltpu.VMEM((2, 31, TILES, LANES), BF16),
        pltpu.VMEM((TILES * PITCH, LANES), F32),
        pltpu.VMEM((16, 8, LANES), F32),
        pltpu.VMEM((16, 8, LANES), F32),
        pltpu.VMEM((512, 512), BF16),
        dma((4,)), dma((5,)), dma, dma((2,)), dma, dma((4,)), *[dma] * 6,
        pltpu.SemaphoreType.REGULAR((3,)),
    ]
    return pl.pallas_call(
        kernel,
        out_shape=jax.ShapeDtypeStruct((16, 512), F32),
        in_specs=[pl.BlockSpec(memory_space=pltpu.HBM)] * 5,
        out_specs=pl.BlockSpec(memory_space=pltpu.VMEM),
        scratch_shapes=scratch,
        compiler_params=pltpu.CompilerParams(
            collective_id=0, has_side_effects=True, vmem_limit_bytes=56418304
        ),
    )(hidden, grad_out, proj_in, proj_out, queries)


def solution(mesh):
    placed = (
        P("dp", "tensor"),
        P(("dp", "tensor"), None),
        P(None, "tensor"),
        P(),
        P(("dp", "tensor"), None),
    )
    return jax.shard_map(
        body, mesh=mesh, in_specs=placed, out_specs=P(("dp", "tensor"), None), check_vma=False
    )
```

time: 229 us -> 30 us (0.13)
  waiting for transfers between devices: 175 us -> 0 us
  Pallas kernels: 0 us -> 29.3 us
  blocking collectives: 24.4 us -> 0 us
  between operations: 13.4 us -> 0.01 us
  matrix products: 11.8 us -> 0 us
    all_gather x1 -> x0, waiting for transfers between devices: 93.3 us -> none  [body(): lax.all_gather(features, 'dp', axis=0, tiled=True)]
    psum x1 -> x0, waiting for transfers between devices: 81.6 us -> none  [body(): summed = lax.psum(outer_sums, 'tensor')]
    pallas_call x0 -> x1, Pallas kernels: none -> 29.3 us  [body(): pl.pallas_call(kernel, out_shape=jax.ShapeDtypeStruct((16, 512), F32), in...]
    all_gather x1 -> x0, blocking collectives: 24.4 us -> none  [body(): gathered = lax.all_gather(local_out, 'tensor', axis=0, tiled=True)]
    dot_general x4 -> x0, matrix products: 11.8 us -> none  [the longest x1 5.43 us: body(): partial_in = jnp.dot(hidden, proj_in.T, preferred_element_type=jnp.float32)]
  transfers between devices with their start and end apart: 2 -> 0, of which waited for: 2 -> 0; matrix products, arithmetic and copies ran while one was open for 0% -> 0% of each run, Pallas kernels for 0% -> 0%
where the time goes in v3:
time: 30 us; the launch traced here: 29.9 us
  Pallas kernels  29.3 us (98%)
  local copies, waits for them, and re-layouts  0.62 us (2%)
    pallas_call x1, Pallas kernels, body(): pl.pallas_call(kernel, out_shape=jax.ShapeDtypeStruct((16, 512), F32), in...  29.3 us
    unnamed x1, local copies, waits for them, and re-layouts  0.62 us

profile of v3, /device:TPU:1, one launch (start us, length us, event | category | flops | bytes accessed | tf_op | source)
XLA Modules:
  0.0 29.9 jit_solution(2403581334537295067)
XLA Ops:
  0.0 29.3 %shard_map.55 = f32[16,512]{1,0:T(8,128)S(1)} custom-call(bf16[2048,1792]{1,0:T(8,128)(2,1)} %hidden.1, bf16[256,4096]{1,0:T(8,128)(2,1)} %grad_out.1, bf16[64,1792]{1,0:T(8,128)(2,1)} %proj_in.1, bf16[64,4096]{1,0:T(8,128)(2,1)} %proj_out.1, bf16[16,4096]{1,0:T(8,128)(2,1)} %queries.1), custom_call_target="tpu_custom_call" | custom-call | tf_op jit(solution)/shard_map/pallas_call | solution.py:308
  29.3 0.6 %copy.7 = f32[16,512]{1,0:T(8,128)} copy(f32[16,512]{1,0:T(8,128)S(1)} %shard_map.55) | data formatting | bytes 65536

commit v4 on v3

--- a/solution.py
+++ b/solution.py
@@ -17,7 +17,8 @@
 PITCH = 72
 
 ORDER = (5, 4, 3, 7, 2, 6, 1, 0)
-STEPS = ((0, ORDER[:4]), (0, ORDER[4:]), (1, ORDER[:4]), (1, ORDER[4:]))
+STEPS = ((0, ORDER[:4]), (0, ORDER[4:]), (1, ORDER[:3]), (1, ORDER[3:6]), (1, ORDER[6:]))
+FIRST = (0, 4, 8, 11, 14)
 SLOTS = ((0, 0), (0, 1), (1, 0), (3, 0), (1, 1), (3, 1), (2, 0), (2, 1))
 
 
@@ -90,7 +91,7 @@
         s, ks = STEPS[step]
         for n, k in enumerate(ks):
             rows = pl.ds(pl.multiple_of(flip(t, k, 3) * 256 + s * SEQ, SEQ), SEQ)
-            pltpu.make_async_copy(hidden.at[rows], x_v.at[step, n], x_sem.at[step]).start()
+            pltpu.make_async_copy(hidden.at[rows], x_v.at[FIRST[step] + n], x_sem.at[step]).start()
 
     load_q.start()
     load_o.start()
@@ -105,7 +106,7 @@
         for peer in greeted:
             tell(barrier, peer)
 
-    for step in range(1, 4):
+    for step in range(1, len(STEPS)):
         load_step(step)
     load_wo.start()
     load_g.start()
@@ -130,8 +131,9 @@
 
     def project(step):
         s, ks = STEPS[step]
-        settle(x_v.at[step], x_sem.at[step])
-        parts = dot_nt(wi_v[...], x_v[step].reshape(4 * SEQ, FF_PART))
+        rows = pl.ds(FIRST[step], len(ks))
+        settle(x_v.at[rows], x_sem.at[step])
+        parts = dot_nt(wi_v[...], x_v[rows].reshape(len(ks) * SEQ, FF_PART))
         for n, k in enumerate(ks):
             part = parts[:, n * SEQ : (n + 1) * SEQ]
             if k:
@@ -155,18 +157,17 @@
     with jax.named_scope("hidden_2"):
         project(2)
         send_parts(2)
-    with jax.named_scope("hidden_3"):
-        project(3)
-        send_parts(3)
-
     with jax.named_scope("heard_1"):
         pl.semaphore_wait(wave.at[1], 4)
         for dz in (4, 3, 5):
             tell(wave.at[2], at(*ahead(0, dz)))
-    with jax.named_scope("query_2"):
-        settle(q_v.at[1], q_rs.at[0])
-        remote(q_v.at[1], q_v.at[5], q_ss, q_rs.at[2], tc_peer(0, 1, 0)).start()
-        remote(q_v.at[1], q_v.at[4], q_ss, q_rs.at[2], tc_peer(0, 3, 0)).start()
+    with jax.named_scope("hidden_3"):
+        project(3)
+        send_parts(3)
+    with jax.named_scope("hidden_4"):
+        project(4)
+        send_parts(4)
+
     with jax.named_scope("grad_part"):
         load_wo.wait()
         load_g.wait()
@@ -187,7 +188,7 @@
             lo = (pin - hi.astype(F32)).astype(BF16)
             right = pout[:, s * SEQ : (s + 1) * SEQ]
             twice = jnp.concatenate([right, right], axis=0)
-            r_v[...] = (dot_nt(hi, twice) + dot_nt(lo, twice)) * (SEQ ** -0.5)
+            r_v[:RANK] = (dot_nt(hi, twice) + dot_nt(lo, twice)) * (SEQ ** -0.5)
             left = lax.broadcasted_iota(jnp.int32, (RANK // 2, LANES), 1) < RANK
             even, odd = r_v[pl.ds(0, 32, stride=2), :], r_v[pl.ds(1, 32, stride=2), :]
             f = jnp.where(left, even, odd).astype(BF16)
@@ -198,6 +199,10 @@
                 src = f_send.at[s, lax.rem(xl + dx, 2)]
                 remote(src, f_recv.at[s, n], f_ss, f_rs, at(*ahead(dx, dz))).start()
 
+    with jax.named_scope("query_2"):
+        settle(q_v.at[1], q_rs.at[0])
+        remote(q_v.at[1], q_v.at[5], q_ss, q_rs.at[2], tc_peer(0, 1, 0)).start()
+        remote(q_v.at[1], q_v.at[4], q_ss, q_rs.at[2], tc_peer(0, 3, 0)).start()
     features(0)
     features(1)
     with jax.named_scope("query_3"):
@@ -287,7 +292,7 @@
 def body(hidden, grad_out, proj_in, proj_out, queries):
     dma = pltpu.SemaphoreType.DMA
     scratch = [
-        pltpu.VMEM((4, 4, SEQ, FF_PART), BF16),
+        pltpu.VMEM((16, SEQ, FF_PART), BF16),
         pltpu.VMEM((256, D), BF16),
         pltpu.VMEM((RANK, FF_PART), BF16),
         pltpu.VMEM((RANK, D), BF16),
@@ -295,14 +300,14 @@
         pltpu.VMEM((16, HALF_K), BF16),
         pltpu.VMEM((2, 8, RANK, SEQ), BF16),
         pltpu.VMEM((2, 8, RANK, SEQ), BF16),
-        pltpu.VMEM((RANK, LANES), F32),
+        pltpu.VMEM((RANK + 8, LANES), F32),
         pltpu.VMEM((2, 2, TILES, LANES), BF16),
         pltpu.VMEM((2, 31, TILES, LANES), BF16),
-        pltpu.VMEM((TILES * PITCH, LANES), F32),
+        pltpu.VMEM(((TILES + 1) * PITCH, LANES), F32),
         pltpu.VMEM((16, 8, LANES), F32),
         pltpu.VMEM((16, 8, LANES), F32),
         pltpu.VMEM((512, 512), BF16),
-        dma((4,)), dma((5,)), dma, dma((2,)), dma, dma((4,)), *[dma] * 6,
+        dma((5,)), dma((5,)), dma, dma((2,)), dma, dma((4,)), *[dma] * 6,
         pltpu.SemaphoreType.REGULAR((3,)),
     ]
     return pl.pallas_call(

time: 30 us -> 29.4 us (0.980)
  Pallas kernels: 29.3 us -> 28.7 us
    pallas_call x1, Pallas kernels: 29.3 us -> 28.7 us  [body(): pl.pallas_call(kernel, out_shape=jax.ShapeDtypeStruct((16, 512), F32), in...]
where the time goes in v4:
time: 29.4 us; the launch traced here: 29.3 us
  Pallas kernels  28.7 us (98%)
  local copies, waits for them, and re-layouts  0.62 us (2%)
    pallas_call x1, Pallas kernels, body(): pl.pallas_call(kernel, out_shape=jax.ShapeDtypeStruct((16, 512), F32), in...  28.7 us
    unnamed x1, local copies, waits for them, and re-layouts  0.62 us

profile of v4, /device:TPU:1, one launch (start us, length us, event | category | flops | bytes accessed | tf_op | source)
XLA Modules:
  0.0 29.3 jit_solution(11587082643297845438)
XLA Ops:
  0.0 28.7 %shard_map.55 = f32[16,512]{1,0:T(8,128)S(1)} custom-call(bf16[2048,1792]{1,0:T(8,128)(2,1)} %hidden.1, bf16[256,4096]{1,0:T(8,128)(2,1)} %grad_out.1, bf16[64,1792]{1,0:T(8,128)(2,1)} %proj_in.1, bf16[64,4096]{1,0:T(8,128)(2,1)} %proj_out.1, bf16[16,4096]{1,0:T(8,128)(2,1)} %queries.1), custom_call_target="tpu_custom_call" | custom-call | tf_op jit(solution)/shard_map/pallas_call | solution.py:313
  28.7 0.6 %copy.7 = f32[16,512]{1,0:T(8,128)} copy(f32[16,512]{1,0:T(8,128)S(1)} %shard_map.55) | data formatting | bytes 65536

commit v5 on v4

--- a/solution.py
+++ b/solution.py
@@ -250,15 +250,24 @@
         right = jnp.concatenate(
             [feats[i * PITCH : i * PITCH + 64, :].astype(BF16) for i in range(TILES)], axis=1
         )
-        scores = dot_nt(q_v[...].reshape(256, HALF_K), right) * (1.0 / RANK)
-        scores = scores.reshape(16, 2, 8, 64)
-        s_send[...] = jnp.concatenate([scores[:, 0], scores[:, 1]], axis=2)
-
-    with jax.named_scope("score_send"):
-        for b, dy, kx in tc_all:
-            slot = b * 8 + SLOTS.index((dy, kx))
-            there = b * 8 + SLOTS.index(((4 - dy) % 4, kx))
-            remote(s_send.at[slot], s_recv.at[there], s_ss, s_rs, tc_peer(b, dy, kx)).start()
+
+    for first in (4, 0):
+        with jax.named_scope("score_part"):
+            rows = jnp.concatenate([q_v[first : first + 4], q_v[first + 8 : first + 12]], axis=0)
+            scores = dot_nt(rows.reshape(128, HALF_K), right) * (1.0 / RANK)
+            scores = scores.reshape(8, 2, 8, 64)
+            packed = jnp.concatenate([scores[:, 0], scores[:, 1]], axis=2)
+            s_send[first : first + 4] = packed[:4]
+            s_send[first + 8 : first + 12] = packed[4:]
+        with jax.named_scope("score_send"):
+            for b, dy, kx in tc_all:
+                n = SLOTS.index((dy, kx))
+                there = b * 8 + SLOTS.index(((4 - dy) % 4, kx))
+                if first <= n < first + 4:
+                    remote(
+                        s_send.at[b * 8 + n], s_recv.at[there], s_ss, s_rs, tc_peer(b, dy, kx)
+                    ).start()
+
     with jax.named_scope("score_wait"):
         settle(s_recv.at[pl.ds(1, 15)], s_rs)
     with jax.named_scope("place"):

time: 29.4 us -> 29.3 us (level)
  no operation moved by 1% of the time
where the time goes in v5:
time: 29.3 us; the launch traced here: 29.2 us
  Pallas kernels  28.6 us (98%)
  local copies, waits for them, and re-layouts  0.62 us (2%)
    pallas_call x1, Pallas kernels, body(): pl.pallas_call(kernel, out_shape=jax.ShapeDtypeStruct((16, 512), F32), in...  28.6 us
    unnamed x1, local copies, waits for them, and re-layouts  0.62 us

profile of v5, /device:TPU:1, one launch (start us, length us, event | category | flops | bytes accessed | tf_op | source)
XLA Modules:
  0.0 29.2 jit_solution(3448521103519591961)
XLA Ops:
  0.0 28.6 %shard_map.55 = f32[16,512]{1,0:T(8,128)S(1)} custom-call(bf16[2048,1792]{1,0:T(8,128)(2,1)} %hidden.1, bf16[256,4096]{1,0:T(8,128)(2,1)} %grad_out.1, bf16[64,1792]{1,0:T(8,128)(2,1)} %proj_in.1, bf16[64,4096]{1,0:T(8,128)(2,1)} %proj_out.1, bf16[16,4096]{1,0:T(8,128)(2,1)} %queries.1), custom_call_target="tpu_custom_call" | custom-call | tf_op jit(solution)/shard_map/pallas_call | solution.py:322
  28.6 0.6 %copy.7 = f32[16,512]{1,0:T(8,128)} copy(f32[16,512]{1,0:T(8,128)S(1)} %shard_map.55) | data formatting | bytes 65536
